TPU v7x, 32 devices: a whole 2x2x4 slice. The times are simulated.
32 devices in a mesh: px: 4 (over z), py: 4 (over y, core), lev: 2 (over x).
Axes of the slice: x: 2, y: 2, z: 4, core: 2. Of those that a mesh axis runs over, the one named last changes fastest.
Arguments:
- pressure: float32 [8, 512, 512], P('lev', 'px', 'py'), may hold values from -6 to 6
- wind_east: float32 [8, 512, 512], P('lev', 'px', 'py'), may hold values from -6 to 6
- wind_north: float32 [8, 512, 512], P('lev', 'px', 'py'), may hold values from -6 to 6
- wind_up: float32 [8, 512, 512], P('lev', 'px', 'py'), may hold values from -6 to 6
- stiffness: float32 [8, 512, 512], P('lev', 'px', 'py'), may hold values from 0.3 to 1
- edge_table: int32 [4, 4, 4], replicated, may hold values from 0 to 7
- remap_source: int32 [65536], P(('px', 'py')), may hold values from 0 to 16383
- remap_weight: float32 [65536], P(('px', 'py')), may hold values from 0.25 to 1
- remap_owner: int32 [65536, 1], P(('px', 'py')), may hold values from 0 to 3; in each aligned block of 4096 rows (0 to 4095, 4096 to 8191, ...) at most 2048 rows name the same one
- latlon_cell: int32 [131072], P(('px', 'py')), may hold values from 0 to 2047
Outputs:
- final_pressure: float32 [8, 512, 512], P('lev', 'px', 'py')
- latlon_fields: float32 [4, 8, 32768], P(None, 'lev', ('px', 'py'))
Inputs may be any that keep to these rules, and one draw needn't show every extreme that they name: `remap_owner`: among the 4096 entries of one tile no owner is named more than 2048 times, and in every draw some tile names some owner exactly 2048 times.
All inputs are finite; a program needn't handle non-finite values.
Results may differ from a plain program's by a relative error of at most 0.0003.
Values sent between devices are 32-bit elements; how exact they have to be, the bound alone decides.
A program may use at most 64 MiB of HBM per device.

v0:
```python
import functools

import jax
import jax.numpy as jnp
from jax import lax
from jax.experimental import pallas as pl
from jax.experimental.pallas import tpu as pltpu
from jax.sharding import PartitionSpec as P

SUBSTEPS = 4
A = 0.45
B = 0.3
LANES = 128
BLOCK = 256
MESH = pl.DeviceIdType.MESH


def iota(shape, dim):
    return lax.broadcasted_iota(jnp.int32, shape, dim)


def parts2(x):
    high = x.astype(jnp.bfloat16)
    return high, (x - high.astype(jnp.float32)).astype(jnp.bfloat16)


def dot_nt(a, b):
    return lax.dot_general(a, b, (((1,), (1,)), ((), ())), preferred_element_type=jnp.float32)


def opposite(s):
    return (s + 2) & 3


SHIFT = ((-1, 0), (0, -1), (1, 0), (0, 1))
DIAGONAL = ((0, 1), (0, 3), (2, 1), (2, 3))


def whole_kernel(
    sizes,
    edges,
    p_in,
    we_in,
    wn_in,
    wu_in,
    st_in,
    owner_in,
    source_in,
    weight_in,
    cell_in,
    p,
    latlon,
    we,
    wn,
    wu,
    st,
    owner,
    source,
    weight,
    cell,
    table,
    near_send,
    near_recv,
    diag_send,
    diag_recv,
    far_send,
    far_recv,
    own_relay,
    level_send,
    level_recv,
    plane_send,
    plane_recv,
    wu_below,
    flipped_cols,
    ghost_rows,
    p_strips,
    w_strips,
    st_strips,
    slot_source,
    slot_weight,
    split,
    payload,
    arrived,
    total,
    in_sems,
    near_sems,
    diag_sems,
    far_sems,
    level_sems,
    plane_sems,
    wub_sems,
    give_sem,
    take_sem,
):
    n_px, n_py, n_lev = sizes
    levels, tile, _ = p.shape
    last = tile - 1
    loads = [
        pltpu.make_async_copy(src, dst, in_sems.at[k])
        for k, (src, dst) in enumerate(
            (
                (p_in, p),
                (we_in, we),
                (wn_in, wn),
                (st_in, st),
                (wu_in, wu),
                (owner_in, owner),
                (source_in, source),
                (weight_in, weight),
                (cell_in, cell),
            )
        )
    ]
    for load in loads:
        load.start()
    ix, iy, iz = lax.axis_index("px"), lax.axis_index("py"), lax.axis_index("lev")
    has_above, has_below = iz < n_lev - 1, iz > 0

    def place(dx, dy):
        return lax.rem(ix + dx + 2 * n_px, n_px), lax.rem(iy + dy + 2 * n_py, n_py)

    def at(dx, dy):
        x, y = place(dx, dy)
        return {"px": x, "py": y}

    others = {(d, 0) for d in range(1, n_px)}
    for dx, dy in ((0, 1), (0, -1), (0, 2), (0, -2), (1, 1), (1, -1), (-1, 1), (-1, -1)):
        others.add((dx % n_px, dy % n_py))
    beside = sorted(o for o in others if o[1])

    barrier = pltpu.get_barrier_semaphore()
    for dx, dy in beside:
        pl.semaphore_signal(barrier, inc=1, device_id=at(dx, dy), device_id_type=MESH)

    def greet(d, carry):
        pl.semaphore_signal(barrier, inc=1, device_id={"px": lax.rem(ix + d, n_px)}, device_id_type=MESH)
        return carry

    lax.fori_loop(1, n_px, greet, 0)

    @pl.when(has_above)
    def _():
        pl.semaphore_signal(barrier, inc=1, device_id={"lev": iz + 1}, device_id_type=MESH)

    @pl.when(has_below)
    def _():
        pl.semaphore_signal(barrier, inc=1, device_id={"lev": iz - 1}, device_id_type=MESH)

    def remote(src, dst, sems, index, device):
        return pltpu.make_async_remote_copy(
            src_ref=src,
            dst_ref=dst,
            send_sem=sems.at[(0,) + index],
            recv_sem=sems.at[(1,) + index],
            device_id=device,
            device_id_type=MESH,
        )

    def near_copy(t, s):
        dx, dy = SHIFT[s]
        return remote(near_send.at[t, s], near_recv.at[t, s], near_sems, (t, s), at(-dx, -dy))

    def diag_copy(t, k):
        (ax, ay), (bx, by) = SHIFT[DIAGONAL[k][0]], SHIFT[DIAGONAL[k][1]]
        return remote(diag_send.at[t, k], diag_recv.at[t, k], diag_sems, (t, k), at(-ax - bx, -ay - by))

    def far_copy(t, s):
        dx, dy = SHIFT[s]
        return remote(far_send.at[t, s], far_recv.at[t, s], far_sems, (t, s), at(-2 * dx, -2 * dy))

    def level_copy(t, up):
        return remote(
            level_send.at[t, up],
            level_recv.at[t, up],
            level_sems,
            (t, up),
            {"lev": iz + 1 if up else iz - 1},
        )

    def plane_copy(t, up, first=False):
        src = p_in.at[levels - 1 if up else 0] if first else plane_send.at[t, up]
        return remote(src, plane_recv.at[t, up], plane_sems, (t, up), {"lev": iz + 1 if up else iz - 1})

    def wub_copy():
        return remote(wu_in.at[levels - 1], wu_below, wub_sems, (0,), {"lev": iz + 1})

    row, lane = iota((tile, tile), 0), iota((tile, tile), 1)
    strip_row, strip_lane = iota((2 * levels, tile), 0), iota((2 * levels, tile), 1)
    outer = strip_row < levels

    def d_rows(f):
        return jnp.where(row == last, 0.0, pltpu.roll(f, last, 0)) - jnp.where(
            row == 0, 0.0, pltpu.roll(f, 1, 0)
        )

    def d_lanes(f):
        return jnp.where(lane == last, 0.0, pltpu.roll(f, last, 1)) - jnp.where(
            lane == 0, 0.0, pltpu.roll(f, 1, 1)
        )

    def columns(deep, shallow):
        packed = jnp.zeros((tile, tile), jnp.float32)
        for j, f in enumerate(deep):
            packed = jnp.where((lane >> 2) == j, pltpu.roll(f, 4 * j + 2, 1), packed)
        base = 4 * len(deep)
        for j, f in enumerate(shallow):
            packed = jnp.where((lane >> 1) == base // 2 + j, pltpu.roll(f, base + 2 * j + 1, 1), packed)
        flipped_cols[...] = packed.T

    def column(k):
        return flipped_cols[pl.ds(k, levels, stride=4), :]

    def rim_column(k):
        return flipped_cols[pl.ds(4 * levels + k, levels, stride=2), :]

    def take_strips():
        columns([p[j] for j in range(levels)], [wn[j] for j in range(levels)])
        for s, (a, b) in ((0, (0, 1)), (2, (last, last - 1))):
            p_strips[s, :levels] = p[:, a, :]
            p_strips[s, levels:] = p[:, b, :]
            w_strips[s, :levels] = we[:, a, :]
        for s, (a, b, c) in ((1, (2, 3, 1)), (3, (1, 0, 0))):
            p_strips[s, :levels] = column(a)
            p_strips[s, levels:] = column(b)
            w_strips[s, :levels] = rim_column(c)

    def code(x, y, s):
        c = edges[x, y, s]
        return c & 3, c >> 2

    def wanted(s, turn):
        return (s + 2 + turn) & 3

    def sign(s, turn):
        plus = ((turn + 1) & 3) < 2 if s % 2 == 0 else turn < 2
        return jnp.where(plus, 1.0, -1.0) * (1.0 if s < 2 else -1.0)

    def rim_sign(w):
        return jnp.where(w < 2, 1.0, -1.0) if not isinstance(w, int) else (1.0 if w < 2 else -1.0)

    near_plan = []
    for s in range(4):
        dx, dy = SHIFT[s]
        turn, flip = code(*place(-dx, -dy), s)
        near_plan.append((flip * 4 + wanted(s, turn), sign(s, turn)))

    def relay_plan(s, w, ax, ay):
        turn_a, flip_a = code(*place(ax, ay), s)
        turn_b, flip_b = code(*place(ax + SHIFT[s][0], ay + SHIFT[s][1]), w)
        return (flip_a ^ flip_b) * 4 + wanted(w, turn_b), sign(s, turn_a) * rim_sign(w)

    def relay_to(s, w):
        return relay_plan(s, w, -SHIFT[s][0] - SHIFT[w][0], -SHIFT[s][1] - SHIFT[w][1])

    diag_plan = [(relay_to(a, b), relay_to(b, a)) for a, b in DIAGONAL]
    far_plan = [relay_to(s, s) for s in range(4)]
    own_plan = [relay_to(s, opposite(s)) for s in range(4)]
    mine = [wanted(s, code(ix, iy, s)[0]) for s in range(4)]

    def relayed(t, s):
        found = own_relay[s]
        for k, (a, b) in enumerate(DIAGONAL):
            if s == a:
                found = jnp.where(mine[s] == b, diag_recv[t, k, :levels], found)
            if s == b:
                found = jnp.where(mine[s] == a, diag_recv[t, k, levels:], found)
        return jnp.where(mine[s] == s, far_recv[t, s], found)

    def send_rims(t):
        strips = [p_strips[s] for s in range(4)]
        rims = []
        for s in range(4):
            turned = A * pltpu.roll(strips[s], levels, 0)
            rims.append(jnp.where(outer, w_strips[s] - rim_sign(s) * turned, turned))
        for s in range(4):
            table[s] = rims[s]
            table[4 + s] = jnp.take_along_axis(rims[s], last - strip_lane, axis=1)
        for s in range(4):
            k, sgn = near_plan[s]
            rim = table[k]
            near_send[t, s] = jnp.where(outer, sgn * rim, rim)
            near_copy(t, s).start()
        for k in range(4):
            for half in range(2):
                which, sgn = diag_plan[k][half]
                diag_send[t, k, half * levels : (half + 1) * levels] = sgn * table[which, levels:]
            diag_copy(t, k).start()
        for s in range(4):
            k, sgn = far_plan[s]
            far_send[t, s] = sgn * table[k, levels:]
            far_copy(t, s).start()
        for s in range(4):
            k, sgn = own_plan[s]
            own_relay[s] = sgn * table[k, levels:]
            for up, level in ((1, levels - 1), (0, 0)):
                level_send[t, up, 2 * s : 2 * s + 2] = p_strips[s, pl.ds(level, 2, stride=levels), :]

        @pl.when(has_above)
        def _():
            level_copy(t, 1).start()

        @pl.when(has_below)
        def _():
            level_copy(t, 0).start()

    def corners(s, low, high):
        found = jnp.zeros((2 * levels, tile), jnp.float32)
        for depth in range(2):
            start = depth if s < 2 else last - depth
            for e in range(2):
                for pair, end in ((low, e), (high, last - e)):
                    moved = pltpu.roll(pair[depth ^ e], (end - start) % tile, 1) if end != start else pair[depth ^ e]
                    here = (strip_lane == end) & (outer if depth == 0 else jnp.logical_not(outer))
                    found = jnp.where(here, moved, found)
        return found

    def next_strips(t):
        for s in range(4):
            near_copy(t, s).wait_recv()
        for k in range(4):
            diag_copy(t, k).wait_recv()
        for s in range(4):
            far_copy(t, s).wait_recv()

        @pl.when(has_above)
        def _():
            level_copy(t, 0).wait_recv()

        @pl.when(has_below)
        def _():
            level_copy(t, 1).wait_recv()

        zero = jnp.zeros((levels, tile), jnp.float32)
        ghosts = []
        for s in range(4):
            ghosts.append(near_recv[t, s] + jnp.concatenate([relayed(t, s), zero], axis=0))
        pairs = [(g, pltpu.roll(g, levels, 0)) for g in ghosts]
        for s in range(4):
            low, high = (pairs[1], pairs[3]) if s % 2 == 0 else (pairs[0], pairs[2])
            across = jnp.zeros((2 * levels, tile), jnp.float32)
            for depth in range(2):
                below, above = level_recv[t, 1], level_recv[t, 0]
                k = 2 * s + depth
                across = jnp.where(strip_row == depth * levels, below[k : k + 1], across)
                across = across + jnp.where(strip_row == (depth + 1) * levels - 1, above[k : k + 1], 0.0)
            p_strips[s] = p_strips[s] + st_strips[s] * (
                A * (ghosts[s] + corners(s, low, high)) + (B * B) * across
            )
            w_strips[s] = jnp.where(outer, w_strips[s] + rim_sign(s) * pairs[s][1], 0.0)

    def give_copy(o):
        return pltpu.make_async_remote_copy(
            src_ref=payload.at[o],
            dst_ref=arrived.at[ix],
            send_sem=give_sem.at[o],
            recv_sem=take_sem.at[ix],
            device_id={"px": o},
            device_id_type=MESH,
        )

    def got(o):
        return pltpu.make_async_remote_copy(
            src_ref=payload.at[o],
            dst_ref=arrived.at[o],
            send_sem=give_sem.at[o],
            recv_sem=take_sem.at[o],
            device_id={"px": o},
            device_id_type=MESH,
        )

    w_strips[...] = jnp.zeros(w_strips.shape, jnp.float32)
    ghost_rows[...] = jnp.zeros((tile, tile), jnp.float32)

    @pl.when(jnp.logical_not(has_below))
    def _():
        wu_below[...] = jnp.zeros((tile, tile), jnp.float32)
        level_recv[:, 1] = jnp.zeros((SUBSTEPS, 8, tile), jnp.float32)

    @pl.when(jnp.logical_not(has_above))
    def _():
        level_recv[:, 0] = jnp.zeros((SUBSTEPS, 8, tile), jnp.float32)

    for load in loads[:3]:
        load.wait()
    take_strips()
    pl.semaphore_wait(
        barrier, n_px - 1 + len(beside) + has_above.astype(jnp.int32) + has_below.astype(jnp.int32)
    )
    send_rims(0)

    @pl.when(has_above)
    def _():
        wub_copy().start()
        plane_copy(0, 1, True).start()

    @pl.when(has_below)
    def _():
        plane_copy(0, 0, True).start()

    for load in loads[3:]:
        load.wait()
    columns([st[j] for j in range(levels)], [])
    for s, (a, b) in ((0, (0, 1)), (2, (last, last - 1))):
        st_strips[s, :levels] = st[:, a, :]
        st_strips[s, levels:] = st[:, b, :]
    for s, (a, b) in ((1, (2, 3)), (3, (1, 0))):
        st_strips[s, :levels] = column(a)
        st_strips[s, levels:] = column(b)
    slot_count = payload.shape[2]
    find_slots(n_px, slot_count, owner, source, weight, slot_source, slot_weight)

    def ahead(d):
        return lax.rem(ix + d + 1, n_px)

    def substep(t, carry):
        for j in range(levels):
            we[j] = we[j] - A * d_rows(p[j])
            wn[j] = wn[j] - A * d_lanes(p[j])
        for j in range(levels - 1):
            wu[j] = wu[j] - B * (p[j + 1] - p[j])

        @pl.when(has_above)
        def _():
            wu[levels - 1] = wu[levels - 1] + B * p[levels - 1]

        @pl.when(jnp.logical_not(has_above))
        def _():
            wu[levels - 1] = jnp.zeros((tile, tile), jnp.float32)

        for j in range(1, levels):
            p[j] = p[j] - st[j] * (A * (d_rows(we[j]) + d_lanes(wn[j])) + B * (wu[j] - wu[j - 1]))

        @pl.when(has_below & (t == 0))
        def _():
            wub_copy().wait_recv()

        @pl.when(has_below)
        def _():
            wu_below[...] = wu_below[...] - B * p[0]

        p[0] = p[0] - st[0] * (A * (d_rows(we[0]) + d_lanes(wn[0])) + B * (wu[0] - wu_below[...]))
        take_strips()
        next_strips(t)

        @pl.when(t < SUBSTEPS - 1)
        def _():
            send_rims(t + 1)

        @pl.when(has_above)
        def _():
            plane_copy(t, 0).wait_recv()
            wu[levels - 1] = wu[levels - 1] - B * plane_recv[t, 0]
            p[levels - 1] = p[levels - 1] + (B * B) * (st[levels - 1] * plane_recv[t, 0])

        @pl.when(has_below)
        def _():
            plane_copy(t, 1).wait_recv()
            wu_below[...] = wu_below[...] + B * plane_recv[t, 1]
            p[0] = p[0] + (B * B) * (st[0] * plane_recv[t, 1])

        for s, (a, b) in ((0, (0, 1)), (2, (last, last - 1))):
            p[:, a, :] = p_strips[s, :levels]
            p[:, b, :] = p_strips[s, levels:]
            we[:, a, :] = w_strips[s, :levels]
        for k, (s, half) in enumerate(((3, 1), (3, 0), (1, 0), (1, 1))):
            ghost_rows[pl.ds(k, levels, stride=4), :] = p_strips[s, half * levels : (half + 1) * levels]
        for k, s in enumerate((3, 1)):
            ghost_rows[pl.ds(4 * levels + k, levels, stride=2), :] = w_strips[s, :levels]
        turned = ghost_rows[...].T
        rim = (lane == 0) | (lane == last)
        band = (lane <= 1) | (lane >= last - 1)
        for j in range(levels):
            p[j] = jnp.where(band, pltpu.roll(turned, (tile - 4 * j - 2) % tile, 1), p[j])
            wn[j] = jnp.where(rim, pltpu.roll(turned, (tile - 4 * levels - 2 * j - 1) % tile, 1), wn[j])

        @pl.when((t < SUBSTEPS - 1) & has_above)
        def _():
            plane_send[t + 1, 1] = p[levels - 1]
            plane_copy(t + 1, 1).start()

        @pl.when((t < SUBSTEPS - 1) & has_below)
        def _():
            plane_send[t + 1, 0] = p[0]
            plane_copy(t + 1, 0).start()

        return carry

    lax.fori_loop(0, SUBSTEPS, substep, 0)

    for q, field in enumerate((p, we, wn, wu)):
        split_field(split, field, q)

    def hand_out(d, carry):
        pick(split, slot_source, slot_weight, payload, ahead(d), ahead(d), 0, 4)
        give_copy(ahead(d)).start()
        return carry

    lax.fori_loop(0, n_px - 1, hand_out, 0)
    pick(split, slot_source, slot_weight, arrived, ix, ix, 0, 4)
    total[...] = jnp.zeros(total.shape, jnp.float32)
    land(arrived, cell, ix, total)

    def bring_in(d, carry):
        o = lax.rem(ix + n_px - d - 1, n_px)
        got(o).wait_recv()
        land(arrived, cell, o, total)
        return carry

    lax.fori_loop(0, n_px - 1, bring_in, 0)
    count, groups = 4 * levels, latlon.shape[2] // BLOCK
    for g in range(groups):
        both = total[g * count : (g + 1) * count] + total[(groups + g) * count : (groups + g + 1) * count]
        for q in range(4):
            latlon[q, :, g * BLOCK : (g + 1) * BLOCK] = both[q * levels : (q + 1) * levels]

    def drain(t, carry):
        for s in range(4):
            near_copy(t, s).wait_send()
            diag_copy(t, s).wait_send()
            far_copy(t, s).wait_send()

        @pl.when(has_above)
        def _():
            level_copy(t, 1).wait_send()
            plane_copy(t, 1).wait_send()

        @pl.when(has_below)
        def _():
            level_copy(t, 0).wait_send()
            plane_copy(t, 0).wait_send()

        return carry

    lax.fori_loop(0, SUBSTEPS, drain, 0)

    @pl.when(has_above)
    def _():
        wub_copy().wait_send()

    def sent(d, carry):
        give_copy(ahead(d)).wait_send()
        return carry

    lax.fori_loop(0, n_px - 1, sent, 0)


def find_slots(owner_count, slot_count, owner, source, weight, slot_source, slot_weight):
    rows = owner.shape[0]
    slot_rows = slot_source.shape[0]
    names = owner[...]
    up_to = (iota((LANES, LANES), 0) <= iota((LANES, LANES), 1)).astype(jnp.bfloat16)
    ones = jnp.ones((LANES, LANES), jnp.bfloat16)
    before = (iota((rows, rows), 0) > iota((rows, rows), 1)).astype(jnp.bfloat16)

    def count(o, rank):
        named = names == o
        hot = named.astype(jnp.float32).astype(jnp.bfloat16)
        within = jnp.dot(hot, up_to, preferred_element_type=jnp.float32)
        total = jnp.dot(hot, ones, preferred_element_type=jnp.float32).astype(jnp.bfloat16)
        earlier = jnp.dot(before, total, preferred_element_type=jnp.float32)
        return jnp.where(named, within + earlier - 1.0, rank)

    rank = lax.fori_loop(0, owner_count, count, jnp.zeros(names.shape, jnp.float32))
    slot = names * slot_count + rank.astype(jnp.int32)
    slot_high, slot_low = slot >> 7, slot & (LANES - 1)
    src = source[...]
    w = weight[...]
    w1 = w.astype(jnp.bfloat16).astype(jnp.float32)
    w2 = (w - w1).astype(jnp.bfloat16).astype(jnp.float32)
    w3 = w - w1 - w2
    pieces = [(src >> 7).astype(jnp.float32), (src & (LANES - 1)).astype(jnp.float32), w1, w2, w3]
    high_place, low_place = iota((slot_rows, LANES), 0), iota((LANES, LANES), 0)
    total = jnp.zeros((len(pieces) * slot_rows, LANES), jnp.float32)
    for r in range(rows):
        here = high_place == slot_high[r : r + 1]
        left = jnp.concatenate([jnp.where(here, piece[r : r + 1], 0.0) for piece in pieces], axis=0)
        right = jnp.where(low_place == slot_low[r : r + 1], 1.0, 0.0)
        total += dot_nt(left.astype(jnp.bfloat16), right.astype(jnp.bfloat16))
    part = [total[k * slot_rows : (k + 1) * slot_rows] for k in range(len(pieces))]
    slot_source[...] = (part[0] * LANES + part[1]).astype(jnp.int32)
    slot_weight[...] = part[2] + part[3] + part[4]


def split_field(split, field, q):
    levels, tile, _ = field.shape
    half = tile // 2
    for l in range(levels):
        h, d = parts2(field[l].T)
        at = slice((q * levels + l) * half, (q * levels + l + 1) * half)
        for k, part in enumerate((h[:half], h[half:], d[:half], d[half:])):
            split[at, k * tile : (k + 1) * tile] = part


def pick(split, slot_source, slot_weight, dst, place, o, first, end):
    rows, slot_count = dst.shape[1:]
    tile = split.shape[1] // 4
    half = tile // 2
    width = min(BLOCK, slot_count)
    pieces = width // LANES
    quarter = rows // 4
    at = slice(first * quarter * half, end * quarter * half)

    def joined(ref, b):
        row = o * (slot_count // LANES) + b * pieces
        return jnp.concatenate([ref[pl.ds(row + k, 1), :] for k in range(pieces)], axis=1)

    def step(b, carry):
        src, w = joined(slot_source, b), joined(slot_weight, b)
        x, y = src >> 7, src & (tile - 1)
        line = x + jnp.where(y >= half, tile, 0)
        hot = jnp.where(iota((2 * tile, width), 0) == line, 1.0, 0.0).astype(jnp.bfloat16)
        picked = jnp.dot(
            split[at, :], jnp.concatenate([hot, hot], axis=0), preferred_element_type=jnp.float32
        )
        mask = jnp.where(iota((half, width), 0) == (y & (half - 1)), w, 0.0)
        dst[place, first * quarter : end * quarter, pl.ds(pl.multiple_of(b * width, width), width)] = jnp.sum(
            picked.reshape((end - first) * quarter, half, width) * mask[None], axis=1
        )
        return carry

    lax.fori_loop(0, slot_count // width, step, 0)


def land(arrived, cell, o, total):
    count, slot_count = arrived.shape[1:]
    groups = total.shape[0] // (2 * count)
    width = min(4 * BLOCK, slot_count)

    def step(b, carry):
        at = pl.ds(pl.multiple_of(b * width, width), width)
        row = o * (slot_count // LANES) + b * (width // LANES)
        c = jnp.concatenate([cell[pl.ds(row + k, 1), :] for k in range(width // LANES)], axis=1)
        values = arrived[o, :, at]
        h = values.astype(jnp.bfloat16).astype(jnp.float32)
        group = c >> 8
        spread = [jnp.where(group == g, h, 0.0) for g in range(groups)]
        spread += [jnp.where(group == g, values - h, 0.0) for g in range(groups)]
        hot = jnp.where(iota((BLOCK, width), 0) == (c & (BLOCK - 1)), 1.0, 0.0)
        total[...] += dot_nt(jnp.concatenate(spread, axis=0).astype(jnp.bfloat16), hot.astype(jnp.bfloat16))
        return carry

    lax.fori_loop(0, slot_count // width, step, 0)


def per_device(
    sizes,
    pressure,
    wind_east,
    wind_north,
    wind_up,
    stiffness,
    edge_table,
    remap_source,
    remap_weight,
    remap_owner,
    latlon_cell,
):
    levels, tile, _ = pressure.shape
    owner_count = sizes[0]
    slots = latlon_cell.shape[0]
    slot_count = slots // owner_count
    cell_count = tile * tile // 8
    count = 4 * levels
    rows = remap_source.shape[0] // LANES
    f32, i32 = jnp.float32, jnp.int32
    n = SUBSTEPS
    field = pltpu.VMEM(pressure.shape, f32)
    plane = pltpu.VMEM((tile, tile), f32)
    dma = pltpu.SemaphoreType.DMA
    in_vmem = pl.BlockSpec(memory_space=pltpu.VMEM)
    return pl.pallas_call(
        functools.partial(whole_kernel, sizes),
        out_shape=[
            jax.ShapeDtypeStruct(pressure.shape, f32),
            jax.ShapeDtypeStruct((4, levels, cell_count), f32),
        ],
        in_specs=[pl.BlockSpec(memory_space=pltpu.SMEM)] + [pl.BlockSpec(memory_space=pl.ANY)] * 9,
        out_specs=[in_vmem] * 2,
        scratch_shapes=[
            field,
            field,
            field,
            field,
            pltpu.VMEM((rows, LANES), i32),
            pltpu.VMEM((rows, LANES), i32),
            pltpu.VMEM((rows, LANES), f32),
            pltpu.VMEM((slots // LANES, LANES), i32),
            pltpu.VMEM((8, 2 * levels, tile), f32),
            pltpu.VMEM((n, 4, 2 * levels, tile), f32),
            pltpu.VMEM((n, 4, 2 * levels, tile), f32),
            pltpu.VMEM((n, 4, 2 * levels, tile), f32),
            pltpu.VMEM((n, 4, 2 * levels, tile), f32),
            pltpu.VMEM((n, 4, levels, tile), f32),
            pltpu.VMEM((n, 4, levels, tile), f32),
            pltpu.VMEM((4, levels, tile), f32),
            pltpu.VMEM((n, 2, 8, tile), f32),
            pltpu.VMEM((n, 2, 8, tile), f32),
            pltpu.VMEM((n, 2, tile, tile), f32),
            pltpu.VMEM((n, 2, tile, tile), f32),
            plane,
            plane,
            plane,
            pltpu.VMEM((4, 2 * levels, tile), f32),
            pltpu.VMEM((4, 2 * levels, tile), f32),
            pltpu.VMEM((4, 2 * levels, tile), f32),
            pltpu.VMEM((slots // LANES, LANES), i32),
            pltpu.VMEM((slots // LANES, LANES), f32),
            pltpu.VMEM((count * tile // 2, 4 * tile), jnp.bfloat16),
            pltpu.VMEM((owner_count, count, slot_count), f32),
            pltpu.VMEM((owner_count, count, slot_count), f32),
            pltpu.VMEM((2 * count * (cell_count // BLOCK), BLOCK), f32),
            dma((9,)),
            dma((2, n, 4)),
            dma((2, n, 4)),
            dma((2, n, 4)),
            dma((2, n, 2)),
            dma((2, n, 2)),
            dma((2, 1)),
            dma((owner_count,)),
            dma((owner_count,)),
        ],
        compiler_params=pltpu.CompilerParams(
            collective_id=0, has_side_effects=True, vmem_limit_bytes=60 * 2**20
        ),
    )(
        edge_table,
        pressure,
        wind_east,
        wind_north,
        wind_up,
        stiffness,
        remap_owner.reshape(rows, LANES),
        remap_source.reshape(rows, LANES),
        remap_weight.reshape(rows, LANES),
        latlon_cell.reshape(slots // LANES, LANES),
    )


def solution(mesh):
    field = P("lev", "px", "py")
    entries = P(("px", "py"))
    sizes = (mesh.shape["px"], mesh.shape["py"], mesh.shape["lev"])
    return jax.shard_map(
        functools.partial(per_device, sizes),
        mesh=mesh,
        in_specs=(field,) * 5 + (P(), entries, entries, P(("px", "py"), None), entries),
        out_specs=(field, P(None, "lev", ("px", "py"))),
        check_vma=False,
    )
```

profile of v0, /device:TPU:0, one launch (start us, length us, event | category | flops | bytes accessed | tf_op | source)
XLA Modules:
  0.0 46.2 jit_solution(15635259890151071132)
XLA Ops:
  0.6 43.2 %shard_map.113 = (f32[4,128,128]{2,1,0:T(8,128)}, f32[4,4,2048]{2,1,0:T(4,128)}) custom-call(s32[4,4,4]{2,1,0:T(4,128)} %edges.1, f32[4,128,128]{2,1,0:T(8,128)} %p_in.1, f32[4,128,128]{2,1,0:T(8,128)} %we_in.1, f32[4,128,128]{2,1,0:T(8,128)} %wn_in.1, f32[4,128,128]{2,1,0:T(8,128)} %wu_in.1, f32[4,128,128]{2,1,0:T(8,128)} %st_in.1, s32[32,128]{1,0:T(8,128)} %bitcast.5, ...), custom_call_target="tpu_custom_call" | custom-call | tf_op jit(solution)/shard_map/pallas_call | solution.py:671
  43.8 0.0 copy-start
  43.9 1.7 %copy.14 = f32[4,128,128]{2,1,0:T(8,128)} copy(f32[4,128,128]{2,1,0:T(8,128)} %get-tuple-element.4) | data formatting | bytes 524288
  45.6 0.0 copy-done
  45.6 0.7 %copy.15 = f32[4,4,2048]{2,1,0:T(4,128)} copy(f32[4,4,2048]{2,1,0:T(4,128)S(1)} %copy-done) | data formatting | bytes 262144
Async XLA Ops:
  43.8 1.7 %copy-start = (f32[4,4,2048]{2,1,0:T(4,128)S(1)}, f32[4,4,2048]{2,1,0:T(4,128)}, u32[]{:S(2)}) copy-start(f32[4,4,2048]{2,1,0:T(4,128)} %get-tuple-element.5) | copy-start | bytes 393220
where the time goes:
time: 46.4 us; the launch traced here: 46.2 us
  Pallas kernels  43.2 us (93%)
  local copies, waits for them, and re-layouts  2.36 us (5%)
  between operations  0.65 us (1%)
    pallas_call x1, Pallas kernels, per_device(): pl.pallas_call(functools.partial(whole_kernel, sizes), out_shape=[jax.Sha...  43.2 us
    unnamed x4, local copies, waits for them, and re-layouts  2.36 us

commit v1 on v0

--- a/solution.py
+++ b/solution.py
@@ -78,9 +78,24 @@
     st_strips,
     slot_source,
     slot_weight,
+    pick_hot,
+    pick_mask,
+    land_hot,
     split,
-    payload,
-    arrived,
+    picked_early,
+    picked_first,
+    picked_second,
+    picked_third,
+    payload_early,
+    payload_first,
+    payload_top,
+    payload_second,
+    payload_third,
+    arrived_early,
+    arrived_first,
+    arrived_top,
+    arrived_second,
+    arrived_third,
     total,
     in_sems,
     near_sems,
@@ -115,6 +130,8 @@
         load.start()
     ix, iy, iz = lax.axis_index("px"), lax.axis_index("py"), lax.axis_index("lev")
     has_above, has_below = iz < n_lev - 1, iz > 0
+    payload = (payload_early, payload_first, payload_top, payload_second, payload_third)
+    arrived = (arrived_early, arrived_first, arrived_top, arrived_second, arrived_third)
 
     def place(dx, dy):
         return lax.rem(ix + dx + 2 * n_px, n_px), lax.rem(iy + dy + 2 * n_py, n_py)
@@ -348,22 +365,22 @@
             )
             w_strips[s] = jnp.where(outer, w_strips[s] + rim_sign(s) * pairs[s][1], 0.0)
 
-    def give_copy(o):
+    def give_copy(c, o):
         return pltpu.make_async_remote_copy(
-            src_ref=payload.at[o],
-            dst_ref=arrived.at[ix],
-            send_sem=give_sem.at[o],
-            recv_sem=take_sem.at[ix],
+            src_ref=payload[c].at[o],
+            dst_ref=arrived[c].at[ix],
+            send_sem=give_sem.at[c, o],
+            recv_sem=take_sem.at[c, ix],
             device_id={"px": o},
             device_id_type=MESH,
         )
 
-    def got(o):
+    def got(c, o):
         return pltpu.make_async_remote_copy(
-            src_ref=payload.at[o],
-            dst_ref=arrived.at[o],
-            send_sem=give_sem.at[o],
-            recv_sem=take_sem.at[o],
+            src_ref=payload[c].at[o],
+            dst_ref=arrived[c].at[o],
+            send_sem=give_sem.at[c, o],
+            recv_sem=take_sem.at[c, o],
             device_id={"px": o},
             device_id_type=MESH,
         )
@@ -406,11 +423,63 @@
     for s, (a, b) in ((1, (2, 3)), (3, (1, 0))):
         st_strips[s, :levels] = column(a)
         st_strips[s, levels:] = column(b)
-    slot_count = payload.shape[2]
-    find_slots(n_px, slot_count, owner, source, weight, slot_source, slot_weight)
+    slot_count = payload_first.shape[2]
+    top = levels - 1
+    every = tuple(range(levels))
+    stages = (
+        (picked_early, ((0, 0, top),), [(wu, l) for l in every[:top]]),
+        (picked_first, ((1, 0, levels), (2, levels, levels + 1)), [(we, l) for l in every] + [(wu, top)]),
+        (picked_second, ((3, 0, levels),), [(wn, l) for l in every]),
+        (picked_third, ((4, 0, levels),), [(p, l) for l in every]),
+    )
+    capacity = pick_hot.shape[1]
+    packed = capacity < n_px * slot_count
+    find_slots(n_px, slot_count, packed, owner, source, weight, slot_source, slot_weight)
+    steps = (capacity // LANES - 1).bit_length()
+    if packed:
+        filled = [
+            jnp.sum(jnp.sum((owner[...] == o).astype(jnp.int32), axis=0, keepdims=True), axis=1, keepdims=True)
+            for o in range(n_px)
+        ]
+
+    def part_of(o, found, low, high):
+        if not packed:
+            return found[low:high, pl.ds(pl.multiple_of(o * slot_count, LANES), slot_count)]
+        start, count = jnp.zeros((1, 1), jnp.int32), jnp.zeros((1, 1), jnp.int32)
+        for k, n in enumerate(filled):
+            start = start + jnp.where(k < o, (n + (LANES - 1)) >> 7, 0)
+            count = count + jnp.where(k == o, n, 0)
+        part = found[low:high, :]
+        for k in reversed(range(steps)):
+            width = slot_count + ((1 << k) - 1) * LANES
+            part = jnp.where(
+                ((start >> k) & 1) == 1, part[:, LANES << k : (LANES << k) + width], part[:, :width]
+            )
+        return jnp.where(iota(part.shape, 1) < count, part, 0.0)
 
     def ahead(d):
         return lax.rem(ix + d + 1, n_px)
+
+    def hand_over(k):
+        found, parts, planes = stages[k]
+        first = sum(len(stage[2]) for stage in stages[:k])
+        for n, (field, l) in enumerate(planes):
+            split_plane(split, field[l], first + n)
+        pick(first, split, pick_hot, pick_mask, found)
+
+        def lay_out(o):
+            whole = part_of(o, found, 0, len(planes))
+            for c, low, high in parts:
+                payload[c][o] = whole[low:high]
+
+        def send(d, carry):
+            lay_out(ahead(d))
+            for c, _, _ in parts:
+                give_copy(c, ahead(d)).start()
+            return carry
+
+        lax.fori_loop(0, n_px - 1, send, 0)
+        lay_out(ix)
 
     def substep(t, carry):
         for j in range(levels):
@@ -440,6 +509,23 @@
 
         p[0] = p[0] - st[0] * (A * (d_rows(we[0]) + d_lanes(wn[0])) + B * (wu[0] - wu_below[...]))
         take_strips()
+
+        @pl.when(t == 1)
+        def _():
+            pick_tables(slot_source, slot_weight, pick_hot, pick_mask)
+            if packed:
+                for found, _, planes in stages:
+                    found[:, capacity:] = jnp.zeros((len(planes), found.shape[1] - capacity), jnp.float32)
+
+        @pl.when(t == 2)
+        def _():
+            land_tables(cell, land_hot)
+            total[...] = jnp.zeros(total.shape, jnp.float32)
+
+        @pl.when(t == SUBSTEPS - 1)
+        def _():
+            hand_over(0)
+
         next_strips(t)
 
         @pl.when(t < SUBSTEPS - 1)
@@ -487,31 +573,28 @@
 
     lax.fori_loop(0, SUBSTEPS, substep, 0)
 
-    for q, field in enumerate((p, we, wn, wu)):
-        split_field(split, field, q)
-
-    def hand_out(d, carry):
-        pick(split, slot_source, slot_weight, payload, ahead(d), ahead(d), 0, 4)
-        give_copy(ahead(d)).start()
-        return carry
-
-    lax.fori_loop(0, n_px - 1, hand_out, 0)
-    pick(split, slot_source, slot_weight, arrived, ix, ix, 0, 4)
-    total[...] = jnp.zeros(total.shape, jnp.float32)
-    land(arrived, cell, ix, total)
-
-    def bring_in(d, carry):
-        o = lax.rem(ix + n_px - d - 1, n_px)
-        got(o).wait_recv()
-        land(arrived, cell, o, total)
-        return carry
-
-    lax.fori_loop(0, n_px - 1, bring_in, 0)
-    count, groups = 4 * levels, latlon.shape[2] // BLOCK
-    for g in range(groups):
-        both = total[g * count : (g + 1) * count] + total[(groups + g) * count : (groups + g + 1) * count]
-        for q in range(4):
-            latlon[q, :, g * BLOCK : (g + 1) * BLOCK] = both[q * levels : (q + 1) * levels]
+    for k in range(1, len(stages)):
+        hand_over(k)
+
+    groups = latlon.shape[2] // BLOCK
+    sums = ((3, (0, 2)), (1, (1,)), (2, (3,)), (0, (4,)))
+
+    for q, parts in sums:
+        land(q, [payload[c][ix] for c in parts], cell, land_hot, ix, total)
+
+    for q, parts in sums:
+
+        def bring_in(d, carry):
+            o = lax.rem(ix + n_px - d - 1, n_px)
+            for c in parts:
+                got(c, o).wait_recv()
+            land(q, [arrived[c][o] for c in parts], cell, land_hot, o, total)
+            return carry
+
+        lax.fori_loop(0, n_px - 1, bring_in, 0)
+        for g in range(groups):
+            high, low = g * levels, (groups + g) * levels
+            latlon[q, :, g * BLOCK : (g + 1) * BLOCK] = total[q, high : high + levels] + total[q, low : low + levels]
 
     def drain(t, carry):
         for s in range(4):
@@ -538,13 +621,14 @@
         wub_copy().wait_send()
 
     def sent(d, carry):
-        give_copy(ahead(d)).wait_send()
+        for c in range(len(payload)):
+            give_copy(c, ahead(d)).wait_send()
         return carry
 
     lax.fori_loop(0, n_px - 1, sent, 0)
 
 
-def find_slots(owner_count, slot_count, owner, source, weight, slot_source, slot_weight):
+def find_slots(owner_count, slot_count, packed, owner, source, weight, slot_source, slot_weight):
     rows = owner.shape[0]
     slot_rows = slot_source.shape[0]
     names = owner[...]
@@ -552,16 +636,24 @@
     ones = jnp.ones((LANES, LANES), jnp.bfloat16)
     before = (iota((rows, rows), 0) > iota((rows, rows), 1)).astype(jnp.bfloat16)
 
-    def count(o, rank):
+    def count(o, carry):
+        place, start = carry
         named = names == o
         hot = named.astype(jnp.float32).astype(jnp.bfloat16)
         within = jnp.dot(hot, up_to, preferred_element_type=jnp.float32)
-        total = jnp.dot(hot, ones, preferred_element_type=jnp.float32).astype(jnp.bfloat16)
-        earlier = jnp.dot(before, total, preferred_element_type=jnp.float32)
-        return jnp.where(named, within + earlier - 1.0, rank)
-
-    rank = lax.fori_loop(0, owner_count, count, jnp.zeros(names.shape, jnp.float32))
-    slot = names * slot_count + rank.astype(jnp.int32)
+        total = jnp.dot(hot, ones, preferred_element_type=jnp.float32)
+        earlier = jnp.dot(before, total.astype(jnp.bfloat16), preferred_element_type=jnp.float32)
+        place = jnp.where(named, within + earlier - 1.0 + start, place)
+        if packed:
+            filled = jnp.sum(total, axis=0, keepdims=True)
+            start = start + jnp.floor((filled + (LANES - 1.0)) / LANES) * LANES
+        else:
+            start = start + float(slot_count)
+        return place, start
+
+    zero = jnp.zeros(names.shape, jnp.float32)
+    place, _ = lax.fori_loop(0, owner_count, count, (zero, jnp.zeros((1, LANES), jnp.float32)))
+    slot = place.astype(jnp.int32)
     slot_high, slot_low = slot >> 7, slot & (LANES - 1)
     src = source[...]
     w = weight[...]
@@ -581,65 +673,77 @@
     slot_weight[...] = part[2] + part[3] + part[4]
 
 
-def split_field(split, field, q):
-    levels, tile, _ = field.shape
+def split_plane(split, plane, r):
+    tile = plane.shape[0]
     half = tile // 2
-    for l in range(levels):
-        h, d = parts2(field[l].T)
-        at = slice((q * levels + l) * half, (q * levels + l + 1) * half)
-        for k, part in enumerate((h[:half], h[half:], d[:half], d[half:])):
-            split[at, k * tile : (k + 1) * tile] = part
-
-
-def pick(split, slot_source, slot_weight, dst, place, o, first, end):
-    rows, slot_count = dst.shape[1:]
-    tile = split.shape[1] // 4
-    half = tile // 2
-    width = min(BLOCK, slot_count)
-    pieces = width // LANES
-    quarter = rows // 4
-    at = slice(first * quarter * half, end * quarter * half)
-
-    def joined(ref, b):
-        row = o * (slot_count // LANES) + b * pieces
-        return jnp.concatenate([ref[pl.ds(row + k, 1), :] for k in range(pieces)], axis=1)
+    h, d = parts2(plane.T)
+    for k, part in enumerate((h[:half], h[half:], d[:half], d[half:])):
+        split[r * half : (r + 1) * half, k * tile : (k + 1) * tile] = part
+
+
+def joined(ref, row, pieces):
+    return jnp.concatenate([ref[pl.ds(row + k, 1), :] for k in range(pieces)], axis=1)
+
+
+def pick_tables(slot_source, slot_weight, pick_hot, pick_mask):
+    lines, capacity = pick_hot.shape
+    tile, half = lines // 2, pick_mask.shape[0]
+    pieces = BLOCK // LANES
 
     def step(b, carry):
-        src, w = joined(slot_source, b), joined(slot_weight, b)
+        at = pl.ds(pl.multiple_of(b * BLOCK, BLOCK), BLOCK)
+        src, w = joined(slot_source, b * pieces, pieces), joined(slot_weight, b * pieces, pieces)
         x, y = src >> 7, src & (tile - 1)
         line = x + jnp.where(y >= half, tile, 0)
-        hot = jnp.where(iota((2 * tile, width), 0) == line, 1.0, 0.0).astype(jnp.bfloat16)
-        picked = jnp.dot(
-            split[at, :], jnp.concatenate([hot, hot], axis=0), preferred_element_type=jnp.float32
-        )
-        mask = jnp.where(iota((half, width), 0) == (y & (half - 1)), w, 0.0)
-        dst[place, first * quarter : end * quarter, pl.ds(pl.multiple_of(b * width, width), width)] = jnp.sum(
-            picked.reshape((end - first) * quarter, half, width) * mask[None], axis=1
-        )
+        pick_hot[:, at] = jnp.where(iota((lines, BLOCK), 0) == line, 1.0, 0.0).astype(jnp.bfloat16)
+        pick_mask[:, at] = jnp.where(iota((half, BLOCK), 0) == (y & (half - 1)), w, 0.0)
         return carry
 
-    lax.fori_loop(0, slot_count // width, step, 0)
-
-
-def land(arrived, cell, o, total):
-    count, slot_count = arrived.shape[1:]
-    groups = total.shape[0] // (2 * count)
-    width = min(4 * BLOCK, slot_count)
+    lax.fori_loop(0, capacity // BLOCK, step, 0)
+
+
+def pick(first, split, pick_hot, pick_mask, found):
+    rows = found.shape[0]
+    half, capacity = pick_mask.shape
+    lines = slice(first * half, (first + rows) * half)
+    width = 2 * BLOCK if capacity % (2 * BLOCK) == 0 else BLOCK
+    steps = capacity // width
 
     def step(b, carry):
         at = pl.ds(pl.multiple_of(b * width, width), width)
-        row = o * (slot_count // LANES) + b * (width // LANES)
-        c = jnp.concatenate([cell[pl.ds(row + k, 1), :] for k in range(width // LANES)], axis=1)
-        values = arrived[o, :, at]
-        h = values.astype(jnp.bfloat16).astype(jnp.float32)
-        group = c >> 8
-        spread = [jnp.where(group == g, h, 0.0) for g in range(groups)]
-        spread += [jnp.where(group == g, values - h, 0.0) for g in range(groups)]
-        hot = jnp.where(iota((BLOCK, width), 0) == (c & (BLOCK - 1)), 1.0, 0.0)
-        total[...] += dot_nt(jnp.concatenate(spread, axis=0).astype(jnp.bfloat16), hot.astype(jnp.bfloat16))
+        hot = pick_hot[:, at]
+        line = jnp.dot(
+            split[lines, :], jnp.concatenate([hot, hot], axis=0), preferred_element_type=jnp.float32
+        )
+        found[:, at] = jnp.sum(line.reshape(rows, half, width) * pick_mask[:, at][None], axis=1)
         return carry
 
-    lax.fori_loop(0, slot_count // width, step, 0)
+    lax.fori_loop(0, steps, step, 0, unroll=steps if steps < 12 else 4)
+
+
+def land_tables(cell, land_hot):
+    owner_count, _, slot_count = land_hot.shape
+    pieces = slot_count // LANES
+
+    def step(o, carry):
+        c = joined(cell, o * pieces, pieces)
+        hot = jnp.where(iota((BLOCK, slot_count), 0) == (c & (BLOCK - 1)), 1.0, 0.0)
+        land_hot[o] = hot.astype(jnp.bfloat16)
+        return carry
+
+    lax.fori_loop(0, owner_count, step, 0)
+
+
+def land(q, parts, cell, land_hot, o, total):
+    values = parts[0] if len(parts) == 1 else jnp.concatenate(parts, axis=0)
+    rows, slot_count = values.shape
+    groups = total.shape[1] // (2 * rows)
+    pieces = slot_count // LANES
+    group = joined(cell, o * pieces, pieces) >> 8
+    h = values.astype(jnp.bfloat16).astype(jnp.float32)
+    spread = [jnp.where(group == g, h, 0.0) for g in range(groups)]
+    spread += [jnp.where(group == g, values - h, 0.0) for g in range(groups)]
+    total[q] += dot_nt(jnp.concatenate(spread, axis=0).astype(jnp.bfloat16), land_hot[o])
 
 
 def per_device(
@@ -661,7 +765,16 @@
     slot_count = slots // owner_count
     cell_count = tile * tile // 8
     count = 4 * levels
-    rows = remap_source.shape[0] // LANES
+    entries = remap_source.shape[0]
+    rows = entries // LANES
+    capacity = -(-(entries + (owner_count - 1) * (LANES - 1)) // BLOCK) * BLOCK
+    capacity = min(capacity, slots)
+    room = capacity
+    if capacity < slots:
+        room = slot_count + ((2 << (capacity // LANES - 1).bit_length() - 1) - 1) * LANES + LANES
+        room = max(room, capacity)
+    slot_rows = -(-capacity // (8 * LANES)) * 8
+    part_rows = (levels - 1, levels, 1, levels, levels)
     f32, i32 = jnp.float32, jnp.int32
     n = SUBSTEPS
     field = pltpu.VMEM(pressure.shape, f32)
@@ -703,12 +816,16 @@
             pltpu.VMEM((4, 2 * levels, tile), f32),
             pltpu.VMEM((4, 2 * levels, tile), f32),
             pltpu.VMEM((4, 2 * levels, tile), f32),
-            pltpu.VMEM((slots // LANES, LANES), i32),
-            pltpu.VMEM((slots // LANES, LANES), f32),
+            pltpu.VMEM((slot_rows, LANES), i32),
+            pltpu.VMEM((slot_rows, LANES), f32),
+            pltpu.VMEM((2 * tile, capacity), jnp.bfloat16),
+            pltpu.VMEM((tile // 2, capacity), f32),
+            pltpu.VMEM((owner_count, BLOCK, slot_count), jnp.bfloat16),
             pltpu.VMEM((count * tile // 2, 4 * tile), jnp.bfloat16),
-            pltpu.VMEM((owner_count, count, slot_count), f32),
-            pltpu.VMEM((owner_count, count, slot_count), f32),
-            pltpu.VMEM((2 * count * (cell_count // BLOCK), BLOCK), f32),
+            *(pltpu.VMEM((n_rows, room), f32) for n_rows in (levels - 1, levels + 1, levels, levels)),
+            *(pltpu.VMEM((owner_count, n_rows, slot_count), f32) for n_rows in part_rows),
+            *(pltpu.VMEM((owner_count, n_rows, slot_count), f32) for n_rows in part_rows),
+            pltpu.VMEM((4, 2 * levels * (cell_count // BLOCK), BLOCK), f32),
             dma((9,)),
             dma((2, n, 4)),
             dma((2, n, 4)),
@@ -716,8 +833,8 @@
             dma((2, n, 2)),
             dma((2, n, 2)),
             dma((2, 1)),
-            dma((owner_count,)),
-            dma((owner_count,)),
+            dma((len(part_rows), owner_count)),
+            dma((len(part_rows), owner_count)),
         ],
         compiler_params=pltpu.CompilerParams(
             collective_id=0, has_side_effects=True, vmem_limit_bytes=60 * 2**20

time: 46.4 us -> 42 us (0.905)
  Pallas kernels: 43.2 us -> 38.8 us
    pallas_call x1, Pallas kernels: 43.2 us -> 38.8 us  [per_device(): pl.pallas_call(functools.partial(whole_kernel, sizes), out_shape=[jax.Sha...]
where the time goes in v1:
time: 42 us; the launch traced here: 41.8 us
  Pallas kernels  38.8 us (92%)
  local copies, waits for them, and re-layouts  2.36 us (6%)
  between operations  0.65 us (2%)
    pallas_call x1, Pallas kernels, per_device(): pl.pallas_call(functools.partial(whole_kernel, sizes), out_shape=[jax.Sha...  38.8 us
    unnamed x4, local copies, waits for them, and re-layouts  2.36 us

profile of v1, /device:TPU:0, one launch (start us, length us, event | category | flops | bytes accessed | tf_op | source)
XLA Modules:
  0.0 41.8 jit_solution(5291580127949451673)
XLA Ops:
  0.6 38.8 %shard_map.113 = (f32[4,128,128]{2,1,0:T(8,128)}, f32[4,4,2048]{2,1,0:T(4,128)}) custom-call(s32[4,4,4]{2,1,0:T(4,128)} %edges.1, f32[4,128,128]{2,1,0:T(8,128)} %p_in.1, f32[4,128,128]{2,1,0:T(8,128)} %we_in.1, f32[4,128,128]{2,1,0:T(8,128)} %wn_in.1, f32[4,128,128]{2,1,0:T(8,128)} %wu_in.1, f32[4,128,128]{2,1,0:T(8,128)} %st_in.1, s32[32,128]{1,0:T(8,128)} %bitcast.5, ...), custom_call_target="tpu_custom_call" | custom-call | tf_op jit(solution)/shard_map/pallas_call | solution.py:784
  39.4 0.0 copy-start
  39.5 1.7 %copy.14 = f32[4,128,128]{2,1,0:T(8,128)} copy(f32[4,128,128]{2,1,0:T(8,128)} %get-tuple-element.4) | data formatting | bytes 524288
  41.2 0.0 copy-done
  41.2 0.7 %copy.15 = f32[4,4,2048]{2,1,0:T(4,128)} copy(f32[4,4,2048]{2,1,0:T(4,128)S(1)} %copy-done) | data formatting | bytes 262144
Async XLA Ops:
  39.4 1.7 %copy-start = (f32[4,4,2048]{2,1,0:T(4,128)S(1)}, f32[4,4,2048]{2,1,0:T(4,128)}, u32[]{:S(2)}) copy-start(f32[4,4,2048]{2,1,0:T(4,128)} %get-tuple-element.5) | copy-start | bytes 393220

commit v2 on v1

--- a/solution.py
+++ b/solution.py
@@ -784,8 +784,8 @@
     return pl.pallas_call(
         functools.partial(whole_kernel, sizes),
         out_shape=[
-            jax.ShapeDtypeStruct(pressure.shape, f32),
-            jax.ShapeDtypeStruct((4, levels, cell_count), f32),
+            pltpu.VMEM(pressure.shape, f32),
+            pltpu.VMEM((4, levels, cell_count), f32),
         ],
         in_specs=[pl.BlockSpec(memory_space=pltpu.SMEM)] + [pl.BlockSpec(memory_space=pl.ANY)] * 9,
         out_specs=[in_vmem] * 2,

time: 42 us -> 40.3 us (0.960)
  local copies, waits for them, and re-layouts: 2.36 us -> 1.36 us
  Pallas kernels: 38.8 us -> 38.1 us
    unnamed x4 -> x2, local copies, waits for them, and re-layouts: 2.36 us -> 1.36 us
    pallas_call x1, Pallas kernels: 38.8 us -> 38.1 us  [per_device(): pl.pallas_call(functools.partial(whole_kernel, sizes), out_shape=[pltpu.V...]
where the time goes in v2:
time: 40.3 us; the launch traced here: 40.1 us
  Pallas kernels  38.1 us (95%)
  local copies, waits for them, and re-layouts  1.36 us (3%)
  between operations  0.64 us (2%)
    pallas_call x1, Pallas kernels, per_device(): pl.pallas_call(functools.partial(whole_kernel, sizes), out_shape=[pltpu.V...  38.1 us
    unnamed x2, local copies, waits for them, and re-layouts  1.36 us

profile of v2, /device:TPU:0, one launch (start us, length us, event | category | flops | bytes accessed | tf_op | source)
XLA Modules:
  0.0 40.1 jit_solution(1435771988656373646)
XLA Ops:
  0.6 38.1 %shard_map.113 = (f32[4,128,128]{2,1,0:T(8,128)S(1)}, f32[4,4,2048]{2,1,0:T(4,128)S(1)}) custom-call(s32[4,4,4]{2,1,0:T(4,128)} %edges.1, f32[4,128,128]{2,1,0:T(8,128)} %p_in.1, f32[4,128,128]{2,1,0:T(8,128)} %we_in.1, f32[4,128,128]{2,1,0:T(8,128)} %wn_in.1, f32[4,128,128]{2,1,0:T(8,128)} %wu_in.1, f32[4,128,128]{2,1,0:T(8,128)} %st_in.1, ...), custom_call_target="tpu_custom_call" | custom-call | tf_op jit(solution)/shard_map/pallas_call | solution.py:784
  38.7 0.7 %copy.14 = f32[4,128,128]{2,1,0:T(8,128)} copy(f32[4,128,128]{2,1,0:T(8,128)S(1)} %get-tuple-element.2) | data formatting | bytes 524288
  39.4 0.7 %copy.15 = f32[4,4,2048]{2,1,0:T(4,128)} copy(f32[4,4,2048]{2,1,0:T(4,128)S(1)} %get-tuple-element.3) | data formatting | bytes 262144

commit v3 on v2

--- a/solution.py
+++ b/solution.py
@@ -12,6 +12,7 @@
 B = 0.3
 LANES = 128
 BLOCK = 256
+EARLY = 2
 MESH = pl.DeviceIdType.MESH
 
 
@@ -38,7 +39,7 @@
 
 def whole_kernel(
     sizes,
-    edges,
+    edges_in,
     p_in,
     we_in,
     wn_in,
@@ -50,6 +51,7 @@
     cell_in,
     p,
     latlon,
+    edges,
     we,
     wn,
     wu,
@@ -76,6 +78,7 @@
     p_strips,
     w_strips,
     st_strips,
+    rim_change,
     slot_source,
     slot_weight,
     pick_hot,
@@ -110,10 +113,46 @@
     n_px, n_py, n_lev = sizes
     levels, tile, _ = p.shape
     last = tile - 1
+    ix, iy, iz = lax.axis_index("px"), lax.axis_index("py"), lax.axis_index("lev")
+    has_above, has_below = iz < n_lev - 1, iz > 0
+    payload = (payload_early, payload_first, payload_top, payload_second, payload_third)
+    arrived = (arrived_early, arrived_first, arrived_top, arrived_second, arrived_third)
+
+    def place(dx, dy):
+        return lax.rem(ix + dx + 2 * n_px, n_px), lax.rem(iy + dy + 2 * n_py, n_py)
+
+    def at(dx, dy):
+        x, y = place(dx, dy)
+        return {"px": x, "py": y}
+
+    others = {(d, 0) for d in range(1, n_px)}
+    for dx, dy in ((0, 1), (0, -1), (0, 2), (0, -2), (1, 1), (1, -1), (-1, 1), (-1, -1)):
+        others.add((dx % n_px, dy % n_py))
+    beside = sorted(o for o in others if o[1])
+
+    barrier = pltpu.get_barrier_semaphore()
+    for dx, dy in beside:
+        pl.semaphore_signal(barrier, inc=1, device_id=at(dx, dy), device_id_type=MESH)
+
+    def greet(d, carry):
+        pl.semaphore_signal(barrier, inc=1, device_id={"px": lax.rem(ix + d, n_px)}, device_id_type=MESH)
+        return carry
+
+    lax.fori_loop(1, n_px, greet, 0)
+
+    @pl.when(has_above)
+    def _():
+        pl.semaphore_signal(barrier, inc=1, device_id={"lev": iz + 1}, device_id_type=MESH)
+
+    @pl.when(has_below)
+    def _():
+        pl.semaphore_signal(barrier, inc=1, device_id={"lev": iz - 1}, device_id_type=MESH)
+
     loads = [
         pltpu.make_async_copy(src, dst, in_sems.at[k])
         for k, (src, dst) in enumerate(
             (
+                (edges_in, edges),
                 (p_in, p),
                 (we_in, we),
                 (wn_in, wn),
@@ -128,41 +167,6 @@
     ]
     for load in loads:
         load.start()
-    ix, iy, iz = lax.axis_index("px"), lax.axis_index("py"), lax.axis_index("lev")
-    has_above, has_below = iz < n_lev - 1, iz > 0
-    payload = (payload_early, payload_first, payload_top, payload_second, payload_third)
-    arrived = (arrived_early, arrived_first, arrived_top, arrived_second, arrived_third)
-
-    def place(dx, dy):
-        return lax.rem(ix + dx + 2 * n_px, n_px), lax.rem(iy + dy + 2 * n_py, n_py)
-
-    def at(dx, dy):
-        x, y = place(dx, dy)
-        return {"px": x, "py": y}
-
-    others = {(d, 0) for d in range(1, n_px)}
-    for dx, dy in ((0, 1), (0, -1), (0, 2), (0, -2), (1, 1), (1, -1), (-1, 1), (-1, -1)):
-        others.add((dx % n_px, dy % n_py))
-    beside = sorted(o for o in others if o[1])
-
-    barrier = pltpu.get_barrier_semaphore()
-    for dx, dy in beside:
-        pl.semaphore_signal(barrier, inc=1, device_id=at(dx, dy), device_id_type=MESH)
-
-    def greet(d, carry):
-        pl.semaphore_signal(barrier, inc=1, device_id={"px": lax.rem(ix + d, n_px)}, device_id_type=MESH)
-        return carry
-
-    lax.fori_loop(1, n_px, greet, 0)
-
-    @pl.when(has_above)
-    def _():
-        pl.semaphore_signal(barrier, inc=1, device_id={"lev": iz + 1}, device_id_type=MESH)
-
-    @pl.when(has_below)
-    def _():
-        pl.semaphore_signal(barrier, inc=1, device_id={"lev": iz - 1}, device_id_type=MESH)
-
     def remote(src, dst, sems, index, device):
         return pltpu.make_async_remote_copy(
             src_ref=src,
@@ -255,6 +259,7 @@
     def rim_sign(w):
         return jnp.where(w < 2, 1.0, -1.0) if not isinstance(w, int) else (1.0 if w < 2 else -1.0)
 
+    loads[0].wait()
     near_plan = []
     for s in range(4):
         dx, dy = SHIFT[s]
@@ -352,6 +357,8 @@
         for s in range(4):
             ghosts.append(near_recv[t, s] + jnp.concatenate([relayed(t, s), zero], axis=0))
         pairs = [(g, pltpu.roll(g, levels, 0)) for g in ghosts]
+        for s in range(2):
+            rim_change[s] = jnp.where(outer, pairs[s][1], -ghosts[s + 2])
         for s in range(4):
             low, high = (pairs[1], pairs[3]) if s % 2 == 0 else (pairs[0], pairs[2])
             across = jnp.zeros((2 * levels, tile), jnp.float32)
@@ -397,7 +404,7 @@
     def _():
         level_recv[:, 0] = jnp.zeros((SUBSTEPS, 8, tile), jnp.float32)
 
-    for load in loads[:3]:
+    for load in loads[1:4]:
         load.wait()
     take_strips()
     pl.semaphore_wait(
@@ -414,7 +421,7 @@
     def _():
         plane_copy(0, 0, True).start()
 
-    for load in loads[3:]:
+    for load in loads[4:]:
         load.wait()
     columns([st[j] for j in range(levels)], [])
     for s, (a, b) in ((0, (0, 1)), (2, (last, last - 1))):
@@ -428,8 +435,8 @@
     every = tuple(range(levels))
     stages = (
         (picked_early, ((0, 0, top),), [(wu, l) for l in every[:top]]),
-        (picked_first, ((1, 0, levels), (2, levels, levels + 1)), [(we, l) for l in every] + [(wu, top)]),
-        (picked_second, ((3, 0, levels),), [(wn, l) for l in every]),
+        (picked_first, ((1, 0, levels),), [(we, l) for l in every]),
+        (picked_second, ((3, 0, levels), (2, levels, levels + 1)), [(wn, l) for l in every] + [(wu, top)]),
         (picked_third, ((4, 0, levels),), [(p, l) for l in every]),
     )
     capacity = pick_hot.shape[1]
@@ -460,12 +467,29 @@
     def ahead(d):
         return lax.rem(ix + d + 1, n_px)
 
-    def hand_over(k):
-        found, parts, planes = stages[k]
+    def choose(k):
+        found, _, planes = stages[k]
         first = sum(len(stage[2]) for stage in stages[:k])
         for n, (field, l) in enumerate(planes):
             split_plane(split, field[l], first + n)
         pick(first, split, pick_hot, pick_mask, found)
+
+    def add_rims(k):
+        found = stages[k][0]
+
+        def step(b, carry):
+            at = pl.ds(pl.multiple_of(b * LANES, LANES), LANES)
+            src = jnp.broadcast_to(slot_source[pl.ds(b, 1), :], (2 * levels, LANES))
+            across, along = (src >> 7, src & last) if k == 1 else (src & last, src >> 7)
+            change = jnp.take_along_axis(rim_change[k - 1], along, axis=1) * slot_weight[pl.ds(b, 1), :]
+            change = jnp.where(across == jnp.where(outer, 0, last), change, 0.0)
+            found[:, at] = found[:, at] + (change[:levels] + change[levels:])
+            return carry
+
+        lax.fori_loop(0, capacity // LANES, step, 0, unroll=4)
+
+    def hand_over(k):
+        found, parts, planes = stages[k]
 
         def lay_out(o):
             whole = part_of(o, found, 0, len(planes))
@@ -524,9 +548,18 @@
 
         @pl.when(t == SUBSTEPS - 1)
         def _():
+            choose(0)
             hand_over(0)
+            for k in range(1, EARLY):
+                choose(k)
 
         next_strips(t)
+
+        @pl.when(t == SUBSTEPS - 1)
+        def _():
+            for k in range(1, EARLY):
+                add_rims(k)
+                hand_over(k)
 
         @pl.when(t < SUBSTEPS - 1)
         def _():
@@ -573,11 +606,12 @@
 
     lax.fori_loop(0, SUBSTEPS, substep, 0)
 
-    for k in range(1, len(stages)):
+    for k in range(EARLY, len(stages)):
+        choose(k)
         hand_over(k)
 
     groups = latlon.shape[2] // BLOCK
-    sums = ((3, (0, 2)), (1, (1,)), (2, (3,)), (0, (4,)))
+    sums = ((1, (1,)), (2, (3,)), (3, (0, 2)), (0, (4,)))
 
     for q, parts in sums:
         land(q, [payload[c][ix] for c in parts], cell, land_hot, ix, total)
@@ -787,9 +821,10 @@
             pltpu.VMEM(pressure.shape, f32),
             pltpu.VMEM((4, levels, cell_count), f32),
         ],
-        in_specs=[pl.BlockSpec(memory_space=pltpu.SMEM)] + [pl.BlockSpec(memory_space=pl.ANY)] * 9,
+        in_specs=[pl.BlockSpec(memory_space=pl.ANY)] * 10,
         out_specs=[in_vmem] * 2,
         scratch_shapes=[
+            pltpu.SMEM(edge_table.shape, i32),
             field,
             field,
             field,
@@ -816,17 +851,18 @@
             pltpu.VMEM((4, 2 * levels, tile), f32),
             pltpu.VMEM((4, 2 * levels, tile), f32),
             pltpu.VMEM((4, 2 * levels, tile), f32),
+            pltpu.VMEM((2, 2 * levels, tile), f32),
             pltpu.VMEM((slot_rows, LANES), i32),
             pltpu.VMEM((slot_rows, LANES), f32),
             pltpu.VMEM((2 * tile, capacity), jnp.bfloat16),
             pltpu.VMEM((tile // 2, capacity), f32),
             pltpu.VMEM((owner_count, BLOCK, slot_count), jnp.bfloat16),
             pltpu.VMEM((count * tile // 2, 4 * tile), jnp.bfloat16),
-            *(pltpu.VMEM((n_rows, room), f32) for n_rows in (levels - 1, levels + 1, levels, levels)),
+            *(pltpu.VMEM((n_rows, room), f32) for n_rows in (levels - 1, levels, levels + 1, levels)),
             *(pltpu.VMEM((owner_count, n_rows, slot_count), f32) for n_rows in part_rows),
             *(pltpu.VMEM((owner_count, n_rows, slot_count), f32) for n_rows in part_rows),
             pltpu.VMEM((4, 2 * levels * (cell_count // BLOCK), BLOCK), f32),
-            dma((9,)),
+            dma((10,)),
             dma((2, n, 4)),
             dma((2, n, 4)),
             dma((2, n, 4)),

time: 40.3 us -> 39.2 us (0.973)
  Pallas kernels: 38.1 us -> 37 us
    pallas_call x1, Pallas kernels: 38.1 us -> 37 us  [per_device(): pl.pallas_call(functools.partial(whole_kernel, sizes), out_shape=[pltpu.V...]
where the time goes in v3:
time: 39.2 us; the launch traced here: 39 us
  Pallas kernels  37 us (94%)
  local copies, waits for them, and re-layouts  1.36 us (3%)
  between operations  0.64 us (2%)
    pallas_call x1, Pallas kernels, per_device(): pl.pallas_call(functools.partial(whole_kernel, sizes), out_shape=[pltpu.V...  37 us
    unnamed x2, local copies, waits for them, and re-layouts  1.36 us

profile of v3, /device:TPU:0, one launch (start us, length us, event | category | flops | bytes accessed | tf_op | source)
XLA Modules:
  0.0 39.0 jit_solution(9709298805949689991)
XLA Ops:
  0.6 37.0 %shard_map.113 = (f32[4,128,128]{2,1,0:T(8,128)S(1)}, f32[4,4,2048]{2,1,0:T(4,128)S(1)}) custom-call(s32[4,4,4]{2,1,0:T(4,128)} %edges_in.1, f32[4,128,128]{2,1,0:T(8,128)} %p_in.1, f32[4,128,128]{2,1,0:T(8,128)} %we_in.1, f32[4,128,128]{2,1,0:T(8,128)} %wn_in.1, f32[4,128,128]{2,1,0:T(8,128)} %wu_in.1, f32[4,128,128]{2,1,0:T(8,128)} %st_in.1, ...), custom_call_target="tpu_custom_call" | custom-call | tf_op jit(solution)/shard_map/pallas_call | solution.py:818
  37.6 0.7 %copy.14 = f32[4,128,128]{2,1,0:T(8,128)} copy(f32[4,128,128]{2,1,0:T(8,128)S(1)} %get-tuple-element.2) | data formatting | bytes 524288
  38.3 0.7 %copy.15 = f32[4,4,2048]{2,1,0:T(4,128)} copy(f32[4,4,2048]{2,1,0:T(4,128)S(1)} %get-tuple-element.3) | data formatting | bytes 262144

commit v4 on v3

--- a/solution.py
+++ b/solution.py
@@ -588,19 +588,28 @@
         turned = ghost_rows[...].T
         rim = (lane == 0) | (lane == last)
         band = (lane <= 1) | (lane >= last - 1)
-        for j in range(levels):
+
+        def put_sides(j):
             p[j] = jnp.where(band, pltpu.roll(turned, (tile - 4 * j - 2) % tile, 1), p[j])
-            wn[j] = jnp.where(rim, pltpu.roll(turned, (tile - 4 * levels - 2 * j - 1) % tile, 1), wn[j])
+
+        put_sides(levels - 1)
 
         @pl.when((t < SUBSTEPS - 1) & has_above)
         def _():
             plane_send[t + 1, 1] = p[levels - 1]
             plane_copy(t + 1, 1).start()
 
+        put_sides(0)
+
         @pl.when((t < SUBSTEPS - 1) & has_below)
         def _():
             plane_send[t + 1, 0] = p[0]
             plane_copy(t + 1, 0).start()
+
+        for j in range(1, levels - 1):
+            put_sides(j)
+        for j in range(levels):
+            wn[j] = jnp.where(rim, pltpu.roll(turned, (tile - 4 * levels - 2 * j - 1) % tile, 1), wn[j])
 
         return carry
 
@@ -611,24 +620,27 @@
         hand_over(k)
 
     groups = latlon.shape[2] // BLOCK
-    sums = ((1, (1,)), (2, (3,)), (3, (0, 2)), (0, (4,)))
-
-    for q, parts in sums:
-        land(q, [payload[c][ix] for c in parts], cell, land_hot, ix, total)
-
-    for q, parts in sums:
+    sums = (((1, 2), (1, 3)), ((3, 0), (0, 2, 4)))
+
+    for n, (_, parts) in enumerate(sums):
+        land(n, [payload[c][ix] for c in parts], cell, land_hot, ix, total)
+
+    for n, (names, parts) in enumerate(sums):
 
         def bring_in(d, carry):
             o = lax.rem(ix + n_px - d - 1, n_px)
             for c in parts:
                 got(c, o).wait_recv()
-            land(q, [arrived[c][o] for c in parts], cell, land_hot, o, total)
+            land(n, [arrived[c][o] for c in parts], cell, land_hot, o, total)
             return carry
 
         lax.fori_loop(0, n_px - 1, bring_in, 0)
         for g in range(groups):
-            high, low = g * levels, (groups + g) * levels
-            latlon[q, :, g * BLOCK : (g + 1) * BLOCK] = total[q, high : high + levels] + total[q, low : low + levels]
+            rows = len(names) * levels
+            high, low = g * rows, (groups + g) * rows
+            both = total[n, high : high + rows] + total[n, low : low + rows]
+            for k, q in enumerate(names):
+                latlon[q, :, g * BLOCK : (g + 1) * BLOCK] = both[k * levels : (k + 1) * levels]
 
     def drain(t, carry):
         for s in range(4):
@@ -815,7 +827,7 @@
     plane = pltpu.VMEM((tile, tile), f32)
     dma = pltpu.SemaphoreType.DMA
     in_vmem = pl.BlockSpec(memory_space=pltpu.VMEM)
-    return pl.pallas_call(
+    results = pl.pallas_call(
         functools.partial(whole_kernel, sizes),
         out_shape=[
             pltpu.VMEM(pressure.shape, f32),
@@ -861,7 +873,7 @@
             *(pltpu.VMEM((n_rows, room), f32) for n_rows in (levels - 1, levels, levels + 1, levels)),
             *(pltpu.VMEM((owner_count, n_rows, slot_count), f32) for n_rows in part_rows),
             *(pltpu.VMEM((owner_count, n_rows, slot_count), f32) for n_rows in part_rows),
-            pltpu.VMEM((4, 2 * levels * (cell_count // BLOCK), BLOCK), f32),
+            pltpu.VMEM((2, 4 * levels * (cell_count // BLOCK), BLOCK), f32),
             dma((10,)),
             dma((2, n, 4)),
             dma((2, n, 4)),
@@ -887,6 +899,24 @@
         remap_weight.reshape(rows, LANES),
         latlon_cell.reshape(slots // LANES, LANES),
     )
+    anywhere = pl.BlockSpec(memory_space=pl.ANY)
+    return pl.pallas_call(
+        pass_on,
+        out_shape=[jax.ShapeDtypeStruct(r.shape, f32) for r in results],
+        in_specs=[in_vmem] * 2,
+        out_specs=[anywhere] * 2,
+        scratch_shapes=[dma((2,))],
+    )(*(pltpu.with_memory_space_constraint(r, pltpu.VMEM) for r in results))
+
+
+def pass_on(p, latlon, p_out, latlon_out, sems):
+    copies = [
+        pltpu.make_async_copy(src, dst, sems.at[k]) for k, (src, dst) in enumerate(((p, p_out), (latlon, latlon_out)))
+    ]
+    for copy in copies:
+        copy.start()
+    for copy in copies:
+        copy.wait()
 
 
 def solution(mesh):

time: 39.2 us -> 38.4 us (0.980)
  local copies, waits for them, and re-layouts: 1.36 us -> 0 us
  Pallas kernels: 37 us -> 37.6 us
    unnamed x2 -> x0, local copies, waits for them, and re-layouts: 1.36 us -> none
    pallas_call x0 -> x1, Pallas kernels: none -> 0.76 us  [per_device(): pl.pallas_call(pass_on, out_shape=[jax.ShapeDtypeStruct(r.shape, f32) for...]
where the time goes in v4:
time: 38.4 us; the launch traced here: 38.2 us
  Pallas kernels  37.6 us (98%)
  between operations  0.64 us (2%)
    pallas_call x1, Pallas kernels, per_device(): pl.pallas_call(functools.partial(whole_kernel, sizes), out_shape=[pltpu.V...  36.8 us

profile of v4, /device:TPU:0, one launch (start us, length us, event | category | flops | bytes accessed | tf_op | source)
XLA Modules:
  0.0 38.2 jit_solution(1173049124087666419)
XLA Ops:
  0.6 36.8 %shard_map.113 = (f32[4,128,128]{2,1,0:T(8,128)S(1)}, f32[4,4,2048]{2,1,0:T(4,128)S(1)}) custom-call(s32[4,4,4]{2,1,0:T(4,128)} %edges_in.1, f32[4,128,128]{2,1,0:T(8,128)} %p_in.1, f32[4,128,128]{2,1,0:T(8,128)} %we_in.1, f32[4,128,128]{2,1,0:T(8,128)} %wn_in.1, f32[4,128,128]{2,1,0:T(8,128)} %wu_in.1, f32[4,128,128]{2,1,0:T(8,128)} %st_in.1, ...), custom_call_target="tpu_custom_call" | custom-call | tf_op jit(solution)/shard_map/pallas_call | solution.py:830
  37.5 0.8 %shard_map.114 = (f32[4,128,128]{2,1,0:T(8,128)}, f32[4,4,2048]{2,1,0:T(4,128)}) custom-call(f32[4,128,128]{2,1,0:T(8,128)S(1)} %get-tuple-element.4.p, f32[4,4,2048]{2,1,0:T(4,128)S(1)} %get-tuple-element.5.latlon), custom_call_target="tpu_custom_call" | custom-call | tf_op jit(solution)/shard_map/pallas_call | solution.py:903

commit v5 on v4

--- a/solution.py
+++ b/solution.py
@@ -78,6 +78,7 @@
     p_strips,
     w_strips,
     st_strips,
+    wu_rims,
     rim_change,
     slot_source,
     slot_weight,
@@ -106,7 +107,6 @@
     far_sems,
     level_sems,
     plane_sems,
-    wub_sems,
     give_sem,
     take_sem,
 ):
@@ -156,8 +156,8 @@
                 (p_in, p),
                 (we_in, we),
                 (wn_in, wn),
+                (wu_in, wu),
                 (st_in, st),
-                (wu_in, wu),
                 (owner_in, owner),
                 (source_in, source),
                 (weight_in, weight),
@@ -198,12 +198,8 @@
             {"lev": iz + 1 if up else iz - 1},
         )
 
-    def plane_copy(t, up, first=False):
-        src = p_in.at[levels - 1 if up else 0] if first else plane_send.at[t, up]
-        return remote(src, plane_recv.at[t, up], plane_sems, (t, up), {"lev": iz + 1 if up else iz - 1})
-
-    def wub_copy():
-        return remote(wu_in.at[levels - 1], wu_below, wub_sems, (0,), {"lev": iz + 1})
+    def plane_copy(t, up):
+        return remote(plane_send.at[t, up], plane_recv.at[t, up], plane_sems, (t, up), {"lev": iz + 1 if up else iz - 1})
 
     row, lane = iota((tile, tile), 0), iota((tile, tile), 1)
     strip_row, strip_lane = iota((2 * levels, tile), 0), iota((2 * levels, tile), 1)
@@ -288,7 +284,7 @@
                 found = jnp.where(mine[s] == a, diag_recv[t, k, levels:], found)
         return jnp.where(mine[s] == s, far_recv[t, s], found)
 
-    def send_rims(t):
+    def send_rims(t, first=False):
         strips = [p_strips[s] for s in range(4)]
         rims = []
         for s in range(4):
@@ -297,16 +293,16 @@
         for s in range(4):
             table[s] = rims[s]
             table[4 + s] = jnp.take_along_axis(rims[s], last - strip_lane, axis=1)
+        for k in range(4):
+            for half in range(2):
+                which, sgn = diag_plan[k][half]
+                diag_send[t, k, half * levels : (half + 1) * levels] = sgn * table[which, levels:]
+            diag_copy(t, k).start()
         for s in range(4):
             k, sgn = near_plan[s]
             rim = table[k]
             near_send[t, s] = jnp.where(outer, sgn * rim, rim)
             near_copy(t, s).start()
-        for k in range(4):
-            for half in range(2):
-                which, sgn = diag_plan[k][half]
-                diag_send[t, k, half * levels : (half + 1) * levels] = sgn * table[which, levels:]
-            diag_copy(t, k).start()
         for s in range(4):
             k, sgn = far_plan[s]
             far_send[t, s] = sgn * table[k, levels:]
@@ -316,6 +312,8 @@
             own_relay[s] = sgn * table[k, levels:]
             for up, level in ((1, levels - 1), (0, 0)):
                 level_send[t, up, 2 * s : 2 * s + 2] = p_strips[s, pl.ds(level, 2, stride=levels), :]
+        if first:
+            level_send[t, 1] = level_send[t, 1] + wu_rims[...] * (1.0 / B)
 
         @pl.when(has_above)
         def _():
@@ -395,33 +393,41 @@
     w_strips[...] = jnp.zeros(w_strips.shape, jnp.float32)
     ghost_rows[...] = jnp.zeros((tile, tile), jnp.float32)
 
+    wu_below[...] = jnp.zeros((tile, tile), jnp.float32)
+
     @pl.when(jnp.logical_not(has_below))
     def _():
-        wu_below[...] = jnp.zeros((tile, tile), jnp.float32)
         level_recv[:, 1] = jnp.zeros((SUBSTEPS, 8, tile), jnp.float32)
 
     @pl.when(jnp.logical_not(has_above))
     def _():
         level_recv[:, 0] = jnp.zeros((SUBSTEPS, 8, tile), jnp.float32)
 
-    for load in loads[1:4]:
+    for load in loads[1:5]:
         load.wait()
+    columns([wu[levels - 1]], [])
+    for k, place_of in enumerate((0, 1, None, None, last, last - 1)):
+        if place_of is not None:
+            wu_rims[k : k + 1] = wu[levels - 1, place_of : place_of + 1, :]
+    for k, place_of in ((2, 2), (3, 3), (6, 1), (7, 0)):
+        wu_rims[k : k + 1] = flipped_cols[place_of : place_of + 1, :]
     take_strips()
+    plane_send[0, 1] = p[levels - 1] + wu[levels - 1] * (1.0 / B)
+    plane_send[0, 0] = p[0]
     pl.semaphore_wait(
         barrier, n_px - 1 + len(beside) + has_above.astype(jnp.int32) + has_below.astype(jnp.int32)
     )
-    send_rims(0)
+    send_rims(0, True)
 
     @pl.when(has_above)
     def _():
-        wub_copy().start()
-        plane_copy(0, 1, True).start()
+        plane_copy(0, 1).start()
 
     @pl.when(has_below)
     def _():
-        plane_copy(0, 0, True).start()
-
-    for load in loads[4:]:
+        plane_copy(0, 0).start()
+
+    for load in loads[5:]:
         load.wait()
     columns([st[j] for j in range(levels)], [])
     for s, (a, b) in ((0, (0, 1)), (2, (last, last - 1))):
@@ -523,10 +529,6 @@
         for j in range(1, levels):
             p[j] = p[j] - st[j] * (A * (d_rows(we[j]) + d_lanes(wn[j])) + B * (wu[j] - wu[j - 1]))
 
-        @pl.when(has_below & (t == 0))
-        def _():
-            wub_copy().wait_recv()
-
         @pl.when(has_below)
         def _():
             wu_below[...] = wu_below[...] - B * p[0]
@@ -661,10 +663,6 @@
         return carry
 
     lax.fori_loop(0, SUBSTEPS, drain, 0)
-
-    @pl.when(has_above)
-    def _():
-        wub_copy().wait_send()
 
     def sent(d, carry):
         for c in range(len(payload)):
@@ -863,6 +861,7 @@
             pltpu.VMEM((4, 2 * levels, tile), f32),
             pltpu.VMEM((4, 2 * levels, tile), f32),
             pltpu.VMEM((4, 2 * levels, tile), f32),
+            pltpu.VMEM((8, tile), f32),
             pltpu.VMEM((2, 2 * levels, tile), f32),
             pltpu.VMEM((slot_rows, LANES), i32),
             pltpu.VMEM((slot_rows, LANES), f32),
@@ -880,7 +879,6 @@
             dma((2, n, 4)),
             dma((2, n, 2)),
             dma((2, n, 2)),
-            dma((2, 1)),
             dma((len(part_rows), owner_count)),
             dma((len(part_rows), owner_count)),
         ],

time: 38.4 us -> 38 us (0.990)
  Pallas kernels: 37.6 us -> 37.2 us
    pallas_call x1, Pallas kernels: 36.8 us -> 36.4 us  [per_device(): pl.pallas_call(functools.partial(whole_kernel, sizes), out_shape=[pltpu.V...]
where the time goes in v5:
time: 38 us; the launch traced here: 37.8 us
  Pallas kernels  37.2 us (98%)
  between operations  0.64 us (2%)
    pallas_call x1, Pallas kernels, per_device(): pl.pallas_call(functools.partial(whole_kernel, sizes), out_shape=[pltpu.V...  36.4 us
    pallas_call x1, Pallas kernels, per_device(): pl.pallas_call(pass_on, out_shape=[jax.ShapeDtypeStruct(r.shape, f32) for...  0.76 us

profile of v5, /device:TPU:0, one launch (start us, length us, event | category | flops | bytes accessed | tf_op | source)
XLA Modules:
  0.0 37.8 jit_solution(7241145498429423847)
XLA Ops:
  0.6 36.4 %shard_map.113 = (f32[4,128,128]{2,1,0:T(8,128)S(1)}, f32[4,4,2048]{2,1,0:T(4,128)S(1)}) custom-call(s32[4,4,4]{2,1,0:T(4,128)} %edges_in.1, f32[4,128,128]{2,1,0:T(8,128)} %p_in.1, f32[4,128,128]{2,1,0:T(8,128)} %we_in.1, f32[4,128,128]{2,1,0:T(8,128)} %wn_in.1, f32[4,128,128]{2,1,0:T(8,128)} %wu_in.1, f32[4,128,128]{2,1,0:T(8,128)} %st_in.1, ...), custom_call_target="tpu_custom_call" | custom-call | tf_op jit(solution)/shard_map/pallas_call | solution.py:828
  37.0 0.8 %shard_map.114 = (f32[4,128,128]{2,1,0:T(8,128)}, f32[4,4,2048]{2,1,0:T(4,128)}) custom-call(f32[4,128,128]{2,1,0:T(8,128)S(1)} %get-tuple-element.4.p, f32[4,4,2048]{2,1,0:T(4,128)S(1)} %get-tuple-element.5.latlon), custom_call_target="tpu_custom_call" | custom-call | tf_op jit(solution)/shard_map/pallas_call | solution.py:901

commit v6 on v5

--- a/solution.py
+++ b/solution.py
@@ -512,11 +512,17 @@
         lay_out(ix)
 
     def substep(t, carry):
+        for j in range(levels - 1):
+            wu[j] = wu[j] - B * (p[j + 1] - p[j])
+
+        @pl.when(t == SUBSTEPS - 1)
+        def _():
+            choose(0)
+            hand_over(0)
+
         for j in range(levels):
             we[j] = we[j] - A * d_rows(p[j])
             wn[j] = wn[j] - A * d_lanes(p[j])
-        for j in range(levels - 1):
-            wu[j] = wu[j] - B * (p[j + 1] - p[j])
 
         @pl.when(has_above)
         def _():
@@ -550,8 +556,6 @@
 
         @pl.when(t == SUBSTEPS - 1)
         def _():
-            choose(0)
-            hand_over(0)
             for k in range(1, EARLY):
                 choose(k)
 

time: 38 us -> 37.7 us (level)
  Pallas kernels: 37.2 us -> 36.8 us
where the time goes in v6:
time: 37.7 us; the launch traced here: 37.5 us
  Pallas kernels  36.8 us (98%)
  between operations  0.64 us (2%)
    pallas_call x1, Pallas kernels, per_device(): pl.pallas_call(functools.partial(whole_kernel, sizes), out_shape=[pltpu.V...  36.1 us
    pallas_call x1, Pallas kernels, per_device(): pl.pallas_call(pass_on, out_shape=[jax.ShapeDtypeStruct(r.shape, f32) for...  0.76 us

profile of v6, /device:TPU:0, one launch (start us, length us, event | category | flops | bytes accessed | tf_op | source)
XLA Modules:
  0.0 37.5 jit_solution(16266917880217222194)
XLA Ops:
  0.6 36.1 %shard_map.113 = (f32[4,128,128]{2,1,0:T(8,128)S(1)}, f32[4,4,2048]{2,1,0:T(4,128)S(1)}) custom-call(s32[4,4,4]{2,1,0:T(4,128)} %edges_in.1, f32[4,128,128]{2,1,0:T(8,128)} %p_in.1, f32[4,128,128]{2,1,0:T(8,128)} %we_in.1, f32[4,128,128]{2,1,0:T(8,128)} %wn_in.1, f32[4,128,128]{2,1,0:T(8,128)} %wu_in.1, f32[4,128,128]{2,1,0:T(8,128)} %st_in.1, ...), custom_call_target="tpu_custom_call" | custom-call | tf_op jit(solution)/shard_map/pallas_call | solution.py:832
  36.7 0.8 %shard_map.114 = (f32[4,128,128]{2,1,0:T(8,128)}, f32[4,4,2048]{2,1,0:T(4,128)}) custom-call(f32[4,128,128]{2,1,0:T(8,128)S(1)} %get-tuple-element.4.p, f32[4,4,2048]{2,1,0:T(4,128)S(1)} %get-tuple-element.5.latlon), custom_call_target="tpu_custom_call" | custom-call | tf_op jit(solution)/shard_map/pallas_call | solution.py:905

commit v7 on v6

--- a/solution.py
+++ b/solution.py
@@ -285,6 +285,20 @@
         return jnp.where(mine[s] == s, far_recv[t, s], found)
 
     def send_rims(t, first=False):
+        for s in range(4):
+            for up, level in ((1, levels - 1), (0, 0)):
+                level_send[t, up, 2 * s : 2 * s + 2] = p_strips[s, pl.ds(level, 2, stride=levels), :]
+        if first:
+            level_send[t, 1] = level_send[t, 1] + wu_rims[...] * (1.0 / B)
+
+        @pl.when(has_above)
+        def _():
+            level_copy(t, 1).start()
+
+        @pl.when(has_below)
+        def _():
+            level_copy(t, 0).start()
+
         strips = [p_strips[s] for s in range(4)]
         rims = []
         for s in range(4):
@@ -310,18 +324,6 @@
         for s in range(4):
             k, sgn = own_plan[s]
             own_relay[s] = sgn * table[k, levels:]
-            for up, level in ((1, levels - 1), (0, 0)):
-                level_send[t, up, 2 * s : 2 * s + 2] = p_strips[s, pl.ds(level, 2, stride=levels), :]
-        if first:
-            level_send[t, 1] = level_send[t, 1] + wu_rims[...] * (1.0 / B)
-
-        @pl.when(has_above)
-        def _():
-            level_copy(t, 1).start()
-
-        @pl.when(has_below)
-        def _():
-            level_copy(t, 0).start()
 
     def corners(s, low, high):
         found = jnp.zeros((2 * levels, tile), jnp.float32)

time: 37.7 us -> 37.7 us (level)
  no operation moved by 1% of the time
where the time goes in v7:
time: 37.7 us; the launch traced here: 37.5 us
  Pallas kernels  36.8 us (98%)
  between operations  0.64 us (2%)
    pallas_call x1, Pallas kernels, per_device(): pl.pallas_call(functools.partial(whole_kernel, sizes), out_shape=[pltpu.V...  36.1 us
    pallas_call x1, Pallas kernels, per_device(): pl.pallas_call(pass_on, out_shape=[jax.ShapeDtypeStruct(r.shape, f32) for...  0.76 us

profile of v7, /device:TPU:0, one launch (start us, length us, event | category | flops | bytes accessed | tf_op | source)
XLA Modules:
  0.0 37.5 jit_solution(11347017244618008033)
XLA Ops:
  0.6 36.1 %shard_map.113 = (f32[4,128,128]{2,1,0:T(8,128)S(1)}, f32[4,4,2048]{2,1,0:T(4,128)S(1)}) custom-call(s32[4,4,4]{2,1,0:T(4,128)} %edges_in.1, f32[4,128,128]{2,1,0:T(8,128)} %p_in.1, f32[4,128,128]{2,1,0:T(8,128)} %we_in.1, f32[4,128,128]{2,1,0:T(8,128)} %wn_in.1, f32[4,128,128]{2,1,0:T(8,128)} %wu_in.1, f32[4,128,128]{2,1,0:T(8,128)} %st_in.1, ...), custom_call_target="tpu_custom_call" | custom-call | tf_op jit(solution)/shard_map/pallas_call | solution.py:834
  36.7 0.8 %shard_map.114 = (f32[4,128,128]{2,1,0:T(8,128)}, f32[4,4,2048]{2,1,0:T(4,128)}) custom-call(f32[4,128,128]{2,1,0:T(8,128)S(1)} %get-tuple-element.4.p, f32[4,4,2048]{2,1,0:T(4,128)S(1)} %get-tuple-element.5.latlon), custom_call_target="tpu_custom_call" | custom-call | tf_op jit(solution)/shard_map/pallas_call | solution.py:907
